TPU v7x, 128 devices: a whole 4x4x4 slice. The times are simulated.
128 devices in a mesh: seq: 2 (over y_lo), ctx: 32 (over y_hi, z, x), wsh: 2 (over core).
Axes of the slice: x: 4, y: 4 (y_hi: 2, y_lo: 2; y = y_hi * 2 + y_lo), z: 4, core: 2. Of those that a mesh axis runs over, the one named last changes fastest.
Arguments:
- tokens: bfloat16 [4, 4096, 768], P(('seq', 'wsh'), 'ctx'), may hold values from -6 to 6
- lengths: int32 [4], P(('seq', 'wsh')), may hold values from 512 to 4096, as said below
- w_query: bfloat16 [768, 768], P('wsh'), may hold values from -0.21875 to 0.21875
- b_query: bfloat16 [768], P('wsh'), may hold values from -3 to 3
- w_key: bfloat16 [768, 768], P('wsh'), may hold values from -0.21875 to 0.21875
- w_value: bfloat16 [768, 768], P('wsh'), may hold values from -0.21875 to 0.21875
- b_value: bfloat16 [768], P('wsh'), may hold values from -3 to 3
- w_out: bfloat16 [768, 768], P('wsh'), may hold values from -6 to 6
- b_out: bfloat16 [768], P('wsh'), may hold values from -3 to 3
- gain_one: bfloat16 [768], P('wsh'), may hold values from 0.5 to 1.5
- shift_one: bfloat16 [768], P('wsh'), may hold values from -3 to 3
- w_up: bfloat16 [768, 3072], P('wsh'), may hold values from -0.21875 to 0.21875
- b_up: bfloat16 [3072], P('wsh'), may hold values from -3 to 3
- w_down: bfloat16 [3072, 768], P('wsh'), may hold values from -0.109375 to 0.109375
- b_down: bfloat16 [768], P('wsh'), may hold values from -3 to 3
- gain_two: bfloat16 [768], P('wsh'), may hold values from 0.5 to 1.5
- shift_two: bfloat16 [768], P('wsh'), may hold values from -3 to 3
- cotangent: bfloat16 [4, 4096, 768], P(('seq', 'wsh'), 'ctx'), may hold values from -6 to 6
Outputs:
- output: bfloat16 [4, 4096, 768], P(('seq', 'wsh'), 'ctx')
- grad_tokens: float32 [4, 4096, 768], P(('seq', 'wsh'), 'ctx')
- grad_w_query: float32 [768, 768], P('wsh')
- grad_b_query: float32 [768], P('wsh')
- grad_w_key: float32 [768, 768], P('wsh')
- grad_w_value: float32 [768, 768], P('wsh')
- grad_b_value: float32 [768], P('wsh')
- grad_w_out: float32 [768, 768], P('wsh')
- grad_b_out: float32 [768], P('wsh')
- grad_gain_one: float32 [768], P('wsh')
- grad_shift_one: float32 [768], P('wsh')
- grad_w_up: float32 [768, 3072], P('wsh')
- grad_b_up: float32 [3072], P('wsh')
- grad_w_down: float32 [3072, 768], P('wsh')
- grad_b_down: float32 [768], P('wsh')
- grad_gain_two: float32 [768], P('wsh')
- grad_shift_two: float32 [768], P('wsh')
Inputs may be any that keep to these rules, and one draw needn't show every extreme that they name: Sequence s has lengths[s] valid tokens at its start, the rest is padding; in every draw some sequence is full, with 4096 valid tokens.
All inputs are finite; a program needn't handle non-finite values.
Results may differ from a plain program's by a relative error of at most 0.024.
Values may be sent and summed in bfloat16 or wider, within the bound.
A program may use at most 192 MiB of HBM per device.

v0:
```python
import math

import jax
import jax.numpy as jnp
from jax import lax
from jax.sharding import Mesh
from jax.sharding import PartitionSpec as P

H = 12
HD = 64
CTX = ("ctx_0", "ctx_1", "ctx_2")
SEQ_CTX = ("seq", "ctx_0", "ctx_1", "ctx_2")


def sent_together(arrays, axis, dim, along):
    widths = [math.prod(a.shape[along:]) for a in arrays]
    both = jnp.concatenate(
        [a.reshape(*a.shape[:along], w) for a, w in zip(arrays, widths)], axis=along
    )
    whole = lax.all_gather(both, axis, axis=dim, tiled=True)
    blocks = jnp.split(whole, [sum(widths[:k]) for k in range(1, len(widths))], axis=along)
    return tuple(
        (b.reshape(*whole.shape[:along], *a.shape[along:]) for a, b in zip(arrays, blocks))
    )


def sent_together_2(arrays, axis, dim, along):
    both = jnp.concatenate(arrays, axis=along)
    whole, at, outs = (lax.all_gather(both, axis, axis=dim, tiled=True), 0, [])
    for a in arrays:
        outs.append(lax.slice_in_dim(whole, at, at + a.shape[along], axis=along))
        at += a.shape[along]
    return tuple(outs)


def sum_in_order(blocks, axes, turns):
    inside = blocks.shape[1:]
    blocks = blocks.reshape(*(lax.axis_size(a) for a in axes), *inside)
    blocks = jnp.moveaxis(blocks, turns, range(len(axes))).reshape(-1, *inside)
    for k in turns:
        blocks = lax.psum_scatter(blocks, axes[k], scatter_dimension=0, tiled=True)
    return blocks[0]


def in_blocks(array, dim, length):
    before, after = (array.shape[:dim], array.shape[dim + 1 :])
    return jnp.moveaxis(array.reshape(*before, length, -1, *after), dim, 0)


def summed_rows(array, axes, turns, dim):
    length = lax.axis_size(axes)
    return sum_in_order(in_blocks(array, dim, length), axes, turns)


def in_one_piece(arrays, axis, dim, along):
    columns = [a.reshape(*a.shape[:along], -1) for a in arrays]
    both = jnp.concatenate(columns, axis=along)
    whole, at, outs = (lax.psum_scatter(both, axis, scatter_dimension=dim, tiled=True), 0, [])
    for a, column in zip(arrays, columns):
        piece = whole[..., at : at + column.shape[along]]
        outs.append(piece.reshape(*piece.shape[:along], *a.shape[along:]))
        at += column.shape[along]
    return tuple(outs)


def layer_norm(resid, gain, shift):
    centre = resid - jnp.mean(resid, axis=-1, keepdims=True)
    spread = jnp.mean(centre * centre, axis=-1, keepdims=True)
    return centre * lax.rsqrt(spread + 1e-12) * gain + shift


def gelu_exact(value):
    return jax.nn.gelu(value, approximate=False)


def local(
    tokens,
    lengths,
    w_query,
    b_query,
    w_key,
    w_value,
    b_value,
    w_out,
    b_out,
    gain_one,
    shift_one,
    w_up,
    b_up,
    w_down,
    b_down,
    gain_two,
    shift_two,
    cotangent,
):
    f32 = jnp.float32
    bf16 = jnp.bfloat16
    wq, bq, wk, wv, bv, wo, bo, gone, sone, wup, bup, wdown, bdown, gtwo, stwo = (
        *sent_together(
            (w_query, b_query, w_key, w_value, b_value, w_out, b_out, gain_one, shift_one, w_up),
            "wsh",
            0,
            1,
        ),
        *sent_together((b_up, w_down), "wsh", 0, 1),
        lax.all_gather(b_down, "wsh", axis=0, tiled=True),
        lax.all_gather(gain_two, "wsh", axis=0, tiled=True),
        lax.all_gather(shift_two, "wsh", axis=0, tiled=True),
    )
    inputs = tokens[0]
    rows = inputs.shape[0]
    width = inputs.shape[1]
    seq_len = lengths[0]
    query = (jnp.dot(inputs, wq, preferred_element_type=f32) + bq.astype(f32)).astype(bf16)
    keys = jnp.dot(inputs, wk, preferred_element_type=f32).astype(bf16)
    values = (jnp.dot(inputs, wv, preferred_element_type=f32) + bv.astype(f32)).astype(bf16)
    query_heads = query.reshape(rows, H, HD)
    pieces = sent_together_2((keys, values), CTX, 0, 1)
    top = jnp.full((H, rows), -1e30, f32)
    count = pieces[0].shape[0]
    valid = (jnp.arange(count) < seq_len)[None, None, :]
    scores = (
        jnp.einsum(
            "qhd,khd->hqk", query_heads, pieces[0].reshape(count, H, HD), preferred_element_type=f32
        )
        * 0.125
    )
    masked = jnp.where(valid, scores, -1e30)
    new_top = jnp.maximum(top, jnp.max(masked, axis=-1))
    expo = jnp.where(valid, jnp.exp(masked - new_top[..., None]), 0.0)
    total = jnp.sum(expo, axis=-1)
    accum = jnp.einsum(
        "hqk,khd->hqd",
        expo.astype(bf16),
        pieces[1].reshape(count, H, HD),
        preferred_element_type=f32,
    )
    top, total, accum = (new_top, total, accum)
    attn_heads = accum / total[..., None]
    log_total = top + jnp.log(total)
    mixed = attn_heads.transpose(1, 0, 2).reshape(rows, width).astype(bf16)
    resid_one = inputs.astype(f32) + jnp.dot(mixed, wo, preferred_element_type=f32) + bo.astype(f32)
    first, pull_one = jax.vjp(layer_norm, resid_one, gone.astype(f32), sone.astype(f32))
    first_low = first.astype(bf16)
    pre = jnp.dot(first_low, wup, preferred_element_type=f32) + bup.astype(f32)
    act, pull_gelu = jax.vjp(gelu_exact, pre)
    act_low = act.astype(bf16)
    resid_two = first + jnp.dot(act_low, wdown, preferred_element_type=f32) + bdown.astype(f32)
    result, pull_two = jax.vjp(layer_norm, resid_two, gtwo.astype(f32), stwo.astype(f32))
    grad_resid_two, grad_gtwo, grad_stwo = pull_two(cotangent[0].astype(f32))
    grad_down_low = grad_resid_two.astype(bf16)
    grad_bdown = jnp.sum(grad_resid_two, axis=0)
    grad_wdown = jnp.einsum("tf,td->fd", act_low, grad_down_low, preferred_element_type=f32)
    grad_act = jnp.einsum("td,fd->tf", grad_down_low, wdown, preferred_element_type=f32)
    grad_pre_low = pull_gelu(grad_act)[0].astype(bf16)
    grad_bup = jnp.sum(grad_pre_low.astype(f32), axis=0)
    grad_wup = jnp.einsum("td,tf->df", first_low, grad_pre_low, preferred_element_type=f32)
    grad_first = grad_resid_two + jnp.einsum(
        "tf,df->td", grad_pre_low, wup, preferred_element_type=f32
    )
    grad_resid_one, grad_gone, grad_sone = pull_one(grad_first)
    grad_branch = grad_resid_one.astype(bf16)
    grad_bout = jnp.sum(grad_resid_one, axis=0)
    grad_wout = jnp.einsum("td,te->de", mixed, grad_branch, preferred_element_type=f32)
    grad_mixed = jnp.einsum("te,de->td", grad_branch, wo, preferred_element_type=f32).astype(bf16)
    grad_heads = grad_mixed.reshape(rows, H, HD)
    delta = jnp.sum(
        grad_mixed.astype(f32).reshape(rows, H, HD).transpose(1, 0, 2) * attn_heads, axis=-1
    )
    pieces = sent_together_2((keys, values), CTX, 0, 1)
    key_piece = pieces[0]
    count = key_piece.shape[0]
    key_heads = key_piece.reshape(count, H, HD)
    value_heads = pieces[1].reshape(count, H, HD)
    valid = (jnp.arange(count) < seq_len)[None, None, :]
    scores = jnp.einsum("qhd,khd->hqk", query_heads, key_heads, preferred_element_type=f32) * 0.125
    probs = jnp.where(valid, jnp.exp(scores - log_total[..., None]), 0.0)
    grad_probs = jnp.einsum("qhd,khd->hqk", grad_heads, value_heads, preferred_element_type=f32)
    grad_scores = (probs * (grad_probs - delta[..., None])).astype(bf16)
    grad_query = (
        jnp.einsum("hqk,khd->qhd", grad_scores, key_heads, preferred_element_type=f32) * 0.125
    )
    grad_keys = (
        jnp.einsum("hqk,qhd->khd", grad_scores, query_heads, preferred_element_type=f32) * 0.125
    )
    grad_values = jnp.einsum(
        "hqk,qhd->khd", probs.astype(bf16), grad_heads, preferred_element_type=f32
    )
    joined = jnp.concatenate(
        [grad_keys.reshape(count, width), grad_values.reshape(count, width)], axis=1
    )
    grad_query, joined = (grad_query, joined)
    pair_grads = joined
    query_sum, pair_grads = (grad_query, pair_grads)
    own_grads = summed_rows(pair_grads.astype(jnp.bfloat16), CTX, (1, 2, 0), 0).astype(jnp.float32)
    grad_query_low = query_sum.reshape(rows, width).astype(bf16)
    grad_keys_low = own_grads[:, :width].astype(bf16)
    grad_values_low = own_grads[:, width:].astype(bf16)
    grad_wq = jnp.einsum("td,te->de", inputs, grad_query_low, preferred_element_type=f32)
    grad_bq = jnp.sum(grad_query_low.astype(f32), axis=0)
    grad_wk = jnp.einsum("td,te->de", inputs, grad_keys_low, preferred_element_type=f32)
    grad_wv = jnp.einsum("td,te->de", inputs, grad_values_low, preferred_element_type=f32)
    grad_bv = jnp.sum(grad_values_low.astype(f32), axis=0)
    grad_inputs = grad_resid_one + jnp.einsum(
        "te,de->td", grad_query_low, wq, preferred_element_type=f32
    )
    grad_inputs = grad_inputs + jnp.einsum(
        "te,de->td", grad_keys_low, wk, preferred_element_type=f32
    )
    grad_inputs = grad_inputs + jnp.einsum(
        "te,de->td", grad_values_low, wv, preferred_element_type=f32
    )
    shares = (
        *tuple(
            (
                part.astype(jnp.float32)
                for part in in_one_piece(
                    (
                        grad_wq.astype(jnp.bfloat16),
                        grad_bq.astype(jnp.bfloat16),
                        grad_wk.astype(jnp.bfloat16),
                        grad_wv.astype(jnp.bfloat16),
                        grad_bv.astype(jnp.bfloat16),
                        grad_wout.astype(jnp.bfloat16),
                        grad_bout.astype(jnp.bfloat16),
                        grad_gone.astype(jnp.bfloat16),
                        grad_sone.astype(jnp.bfloat16),
                        grad_wup.astype(jnp.bfloat16),
                    ),
                    "wsh",
                    0,
                    1,
                )
            )
        ),
        *tuple(
            (
                part.astype(jnp.float32)
                for part in in_one_piece(
                    (grad_bup.astype(jnp.bfloat16), grad_wdown.astype(jnp.bfloat16)), "wsh", 0, 1
                )
            )
        ),
        lax.psum_scatter(
            grad_bdown.astype(jnp.bfloat16), "wsh", scatter_dimension=0, tiled=True
        ).astype(jnp.float32),
        lax.psum_scatter(
            grad_gtwo.astype(jnp.bfloat16), "wsh", scatter_dimension=0, tiled=True
        ).astype(jnp.float32),
        lax.psum_scatter(
            grad_stwo.astype(jnp.bfloat16), "wsh", scatter_dimension=0, tiled=True
        ).astype(jnp.float32),
    )
    totals = lax.psum(
        (
            shares[0],
            shares[1],
            shares[2],
            shares[3],
            shares[4],
            shares[5],
            shares[6],
            shares[7],
            shares[8],
            shares[9],
            shares[10],
            shares[11],
            shares[12],
            shares[13],
            shares[14],
        ),
        SEQ_CTX,
    )
    return (
        result.astype(bf16)[None],
        grad_inputs[None],
        totals[0],
        totals[1],
        totals[2],
        totals[3],
        totals[4],
        totals[5],
        totals[6],
        totals[7],
        totals[8],
        totals[9],
        totals[10],
        totals[11],
        totals[12],
        totals[13],
        totals[14],
    )


def solution(mesh):
    split = Mesh(
        mesh.devices.reshape(mesh.shape["seq"], 2, 4, 4, mesh.shape["wsh"]),
        ("seq", "ctx_0", "ctx_1", "ctx_2", "wsh"),
    )
    return jax.shard_map(
        local,
        mesh=split,
        in_specs=(
            P(("seq", "wsh"), CTX, None),
            P(("seq", "wsh")),
            P("wsh", None),
            P("wsh"),
            P("wsh", None),
            P("wsh", None),
            P("wsh"),
            P("wsh", None),
            P("wsh"),
            P("wsh"),
            P("wsh"),
            P("wsh", None),
            P("wsh"),
            P("wsh", None),
            P("wsh"),
            P("wsh"),
            P("wsh"),
            P(("seq", "wsh"), CTX, None),
        ),
        out_specs=(
            P(("seq", "wsh"), CTX, None),
            P(("seq", "wsh"), CTX, None),
            P("wsh", None),
            P("wsh"),
            P("wsh", None),
            P("wsh", None),
            P("wsh"),
            P("wsh", None),
            P("wsh"),
            P("wsh"),
            P("wsh"),
            P("wsh", None),
            P("wsh"),
            P("wsh", None),
            P("wsh"),
            P("wsh"),
            P("wsh"),
        ),
        check_vma=False,
    )
```

profile of v0, /device:TPU:0, one launch (start us, length us, event | category | flops | bytes accessed | tf_op | source)
XLA Modules:
  0.0 997.0 jit_solution(7318561539436176737)
XLA Ops:
  11.2 9.3 concatenate.25
  22.2 3.0 pad_maximum_fusion.2
  25.3 22.6 %all-gather.7.cloned.1.call-done = bf16[768,6149]{1,0:T(8,128)(2,1)} async-done(((bf16[384,6149]{1,0:T(8,128)(2,1)}), bf16[768,6149]{1,0:T(8,128)(2,1)}) %all-gather.7.cloned.1.call-update) | async-done | bytes 9444880 | tf_op jit(solution)/shard_map/all_gather | solution.py:20
  61.8 8.0 all-gather.11.cloned.1.call-done
  73.0 136.4 %all-gather.9.cloned.1.call-done = bf16[4096,1536]{0,1:T(8,128)(2,1)} async-done(((bf16[128,1536]{0,1:T(8,128)(2,1)}), bf16[4096,1536]{0,1:T(8,128)(2,1)}) %all-gather.9.cloned.1.call-update) | async-done | bytes 12582928 | tf_op jit(solution)/shard_map/all_gather | solution.py:29
  209.4 5.4 fusion.96
  214.9 10.7 %select_reduce_fusion = (f32[12,128]{1,0:T(8,128)S(1)}, f32[12,128,4096]{2,1,0:T(8,128)}) fusion(pred[4096]{0:T(1024)(128)(4,1)S(1)} %iota_compare_fusion, bf16[128,12,64]{0,2,1:T(8,128)(2,1)S(1)} %bitcast.106, bf16[4096,12,64]{0,2,1:T(8,128)(2,1)S(1)} %bitcast.87), kind=kOutput, calls=%fused_computation.3 | convolution fusion | flops 824179200 | bytes 31664128 | tf_op jit(solution)/shard_map/qhd,khd->hqk/dot_general | solution.py:123
  225.5 12.8 %fusion.1 = f32[12,128]{1,0:T(8,128)S(1)} fusion(f32[12,128,4096]{2,1,0:T(8,128)} %get-tuple-element.115, f32[12,128]{1,0:T(8,128)S(1)} %broadcast_maximum_fusion, pred[4096]{0:T(1024)(128)(4,1)S(1)} %iota_compare_fusion), kind=kLoop, calls=%fused_computation.5 | loop fusion | flops 31455744 | bytes 25182208 | tf_op jit(solution)/shard_map/reduce_sum | solution.py:131
  238.4 11.9 %fusion.70 = (bf16[128,12,64]{0,2,1:T(8,128)(2,1)S(1)}, f32[12,128,64]{1,2,0:T(8,128)}) fusion(f32[128,12]{0,1:T(8,128)S(1)} %bitcast.112, bf16[4096,12,64]{0,2,1:T(8,128)(2,1)S(1)} %bitcast.90, f32[12,128,4096]{2,1,0:T(8,128)} %get-tuple-element.115, f32[12,128]{1,0:T(8,128)S(1)} %broadcast_maximum_fusion, pred[4096]{0:T(1024)(128)(4,1)S(1)} %iota_compare_fusion), kind=kOutput, calls=%fused_computation.102 | convolution fusion | flops 836960256 | bytes 32063488 | tf_op jit(solution)/shard_map/hqk,khd->hqd/dot_general | solution.py:132
  252.7 7.5 multiply_convert_fusion.2
  266.5 2.7 multiply_reduce_fusion
  270.5 12.5 %fusion.16 = bf16[4096,12,64]{0,2,1:T(8,128)(2,1)} fusion(bf16[128,12,64]{0,2,1:T(8,128)(2,1)S(1)} %bitcast.97, f32[12,128,4096]{2,1,0:T(8,128)} %get-tuple-element.115, f32[12,128]{1,0:T(8,128)S(1)} %log_add_fusion, pred[4096]{0:T(1024)(128)(4,1)S(1)} %iota_compare_fusion), kind=kOutput, calls=%fused_computation.18 | convolution fusion | flops 833617920 | bytes 31664128 | tf_op jit(solution)/shard_map/hqk,qhd->khd/dot_general | solution.py:186
  283.0 17.4 %multiply_convert_fusion = bf16[12,128,4096]{2,1,0:T(8,128)(2,1)} fusion(f32[12,128,4096]{2,1,0:T(8,128)} %get-tuple-element.115, f32[12,128]{1,0:T(8,128)S(1)} %fusion.69, f32[12,128]{1,0:T(8,128)S(1)} %log_add_fusion, pred[4096]{0:T(1024)(128)(4,1)S(1)} %iota_compare_fusion, bf16[128,12,64]{0,2,1:T(8,128)(2,1)S(1)} %bitcast.98, ...), kind=kOutput, calls=%fused_computation | convolution fusion | flops 843055104 | bytes 44253184 | tf_op jit(solution)/shard_map/qhd,khd->hqk/dot_general | solution.py:178
  300.4 11.0 %concatenate.29 = bf16[2,4,4,128,768]{3,2,1,0,4:T(4,128)(2,1)} reshape(bf16[4096,12,64]{0,2,1:T(8,128)(2,1)} %fusion.16) | data formatting | bytes 12582912 | tf_op jit(solution)/shard_map/concatenate | solution.py:189
  311.4 10.8 %copy.68 = bf16[2,4,4,128,768]{4,3,0,2,1:T(8,128)(2,1)} copy(bf16[2,4,4,128,768]{3,2,1,0,4:T(4,128)(2,1)} %concatenate.29) | data formatting | bytes 12582912 | tf_op jit(solution)/shard_map/concatenate | solution.py:189
  322.1 9.1 fusion.15
  331.2 11.0 %concatenate.28 = bf16[2,4,4,128,768]{3,2,1,0,4:T(4,128)(2,1)} reshape(bf16[4096,12,64]{0,2,1:T(8,128)(2,1)} %fusion.15) | data formatting | bytes 12582912 | tf_op jit(solution)/shard_map/concatenate | solution.py:189
  342.2 10.7 %copy.67 = bf16[2,4,4,128,768]{4,3,0,2,1:T(8,128)(2,1)} copy(bf16[2,4,4,128,768]{3,2,1,0,4:T(4,128)(2,1)} %concatenate.28) | data formatting | bytes 12582912 | tf_op jit(solution)/shard_map/concatenate | solution.py:189
  352.9 12.8 %pad_maximum_fusion = bf16[2,4,4,128,1536]{4,3,0,2,1:T(8,128)(2,1)} fusion(bf16[2,4,4,128,768]{4,3,0,2,1:T(8,128)(2,1)} %copy.68, bf16[2,4,4,128,768]{4,3,0,2,1:T(8,128)(2,1)} %copy.67), kind=kLoop, calls=%fused_computation.8 | loop fusion | flops 25165824 | bytes 25165824 | tf_op jit(solution)/shard_map/concatenate | solution.py:189
  365.8 114.1 %reduce-scatter.6.cloned.1.call-done = bf16[8,128,1536]{2,1,0:T(8,128)(2,1)} async-done(((bf16[32,128,1536]{2,1,0:T(8,128)(2,1)}), bf16[8,128,1536]{2,1,0:T(8,128)(2,1)}) %reduce-scatter.6.cloned.1.call-update) | async-done | bytes 3145744 | tf_op jit(solution)/shard_map/reduce_scatter | solution.py:41
  479.9 40.0 %reduce-scatter.8.cloned.1.call-done = bf16[2,128,1536]{2,1,0:T(8,128)(2,1)} async-done(((bf16[8,128,1536]{2,1,0:T(8,128)(2,1)}), bf16[2,128,1536]{2,1,0:T(8,128)(2,1)}) %reduce-scatter.8.cloned.1.call-update) | async-done | bytes 786448 | tf_op jit(solution)/shard_map/reduce_scatter | solution.py:41
  521.5 3.4 pad_maximum_fusion.1
  525.2 11.2 %bitcast_reduce_fusion = (bf16[12,64]{1,0:T(8,128)(2,1)S(1)}, bf16[12,64,128]{2,1,0:T(8,128)(2,1)S(1)}) fusion(bf16[4096,12,64]{0,2,1:T(8,128)(2,1)} %bitcast.88, bf16[12,128,4096]{2,1,0:T(8,128)(2,1)} %multiply_convert_fusion), kind=kOutput, calls=%fused_computation.120 | convolution fusion | flops 805600512 | bytes 19072512 | tf_op jit(solution)/shard_map/hqk,khd->qhd/dot_general | solution.py:181
  547.9 4.8 convolution_convert_fusion.1
  564.6 17.4 %concatenate.31 = bf16[768,6149]{1,0:T(8,128)(2,1)} concatenate(bf16[768,768]{1,0:T(8,128)(2,1)S(1)} %copy.69, bf16[768,1]{1,0:T(8,128)(2,1)S(1)} %copy-done.14, bf16[768,768]{1,0:T(8,128)(2,1)} %copy.71, bf16[768,768]{1,0:T(8,128)(2,1)} %copy.72, bf16[768,1]{1,0:T(8,128)(2,1)} %reshape.313, bf16[768,768]{1,0:T(8,128)(2,1)S(1)} %copy.74, bf16[768,1]{1,0:T(8,128)(2,1)S(1)} %copy-done.15, ...), dimensions={1} | concatenate | bytes 18889728 | tf_op jit(solution)/shard_map/concatenate | solution.py:57
  582.1 4.6 slice_convert_fusion
  586.7 16.0 %reduce-scatter.12.cloned.1.call-done = bf16[384,6149]{1,0:T(8,128)(2,1)} async-done(((bf16[768,6149]{1,0:T(8,128)(2,1)}), bf16[384,6149]{1,0:T(8,128)(2,1)}) %reduce-scatter.12.cloned.1.call-update) | async-done | bytes 4722448 | tf_op jit(solution)/shard_map/reduce_scatter | solution.py:58
  602.7 4.6 slice_convert_fusion.2
  607.3 4.7 slice_convert_fusion.1
  621.7 3.1 fusion.41
  626.3 350.9 %all-reduce.3 = (f32[384]{0:T(512)}, f32[384]{0:T(512)}, f32[384]{0:T(512)}, f32[384]{0:T(512)}, f32[384]{0:T(512)}, /*index=5*/f32[1536]{0:T(1024)}, f32[384]{0:T(512)}, f32[384]{0:T(512)}, f32[384]{0:T(512)}) all-reduce(f32[384]{0:T(512)S(1)} %get-tuple-element.77, ...), channel_id=1, replica_groups=mesh['seq'=2,'ctx_0'=2,'ctx_1'=4,'ctx_2'=4,'wsh'=2] {'seq','ctx_0','ctx_..., use_global_device_ids=true, to_apply=%region_21.22 | all-reduce | flops 4608 | bytes 36864 | tf_op jit(solution)/shard_map/psum | solution.py:254
  977.2 6.2 copy.78
  (176 shorter events, 74.5 us)
Async XLA Ops:
  7.2 40.7 %all-gather.7.cloned.1.call-start = ((), (), s32[]{:S(2)}) async-start(), calls=%async_computation.5 | async-start | bytes 14450688 | tf_op jit(solution)/shard_map/all_gather | solution.py:20
  20.6 49.2 %all-gather.11.cloned.1.call-start = ((), (), s32[]{:S(2)}) async-start(), calls=%async_computation.7 | async-start | bytes 8257536 | tf_op jit(solution)/shard_map/all_gather | solution.py:20
  25.2 24.6 %copy-start.2 = (bf16[1,128,768]{2,1,0:T(8,128)(2,1)S(1)}, bf16[1,128,768]{2,1,0:T(8,128)(2,1)}, u32[]{:S(2)}) copy-start(bf16[1,128,768]{2,1,0:T(8,128)(2,1)} %param.18) | copy-start | bytes 589828
  25.2 184.2 %all-gather.9.cloned.1.call-start = ((), (), s32[]{:S(2)}) async-start(), calls=%async_computation.6 | async-start | bytes 12976128 | tf_op jit(solution)/shard_map/all_gather | solution.py:29
  49.9 5.5 copy-start.26
  49.9 8.0 copy-start.27
  49.9 9.8 copy-start.28
  55.4 424.5 %reduce-scatter.6.cloned.1.call-start = ((), (), s32[]{:S(2)}) async-start(), calls=%async_computation.8 | async-start | bytes 15728640 | tf_op jit(solution)/shard_map/reduce_scatter | solution.py:41
  214.8 10.7 %copy-start = (bf16[4096,768]{0,1:T(8,128)(2,1)}, bf16[4096,768]{0,1:T(8,128)(2,1)S(1)}, u32[]{:S(2)}) copy-start(bf16[4096,768]{0,1:T(8,128)(2,1)S(1)} %get-tuple-element.107) | copy-start | bytes 18874372
  214.9 23.5 %copy-start.1 = (bf16[4096,768]{0,1:T(8,128)(2,1)}, bf16[4096,768]{0,1:T(8,128)(2,1)S(1)}, u32[]{:S(2)}) copy-start(bf16[4096,768]{0,1:T(8,128)(2,1)S(1)} %get-tuple-element.108) | copy-start | bytes 18874372
  250.3 9.9 copy-start.17
  250.3 9.9 slice-start.5
  252.7 16.6 %copy-start.20 = (f32[128]{0:T(128)}, f32[128]{0:T(128)S(1)}, u32[]{:S(2)}) copy-start(f32[128]{0:T(128)S(1)} %fusion.84) | copy-start | bytes 1540
  252.7 7.5 slice-start.6
  252.7 9.6 copy-start.6
  260.2 6.3 slice-start.2
  260.2 6.3 slice-start.3
  264.0 256.0 %copy-start.24 = (f32[128]{0:T(128)}, f32[128]{0:T(128)S(1)}, u32[]{:S(2)}) copy-start(f32[128]{0:T(128)S(1)} %negate_multiply_fusion.2) | copy-start | bytes 1540
  269.5 13.5 %copy-start.21 = (f32[128]{0:T(128)}, f32[128]{0:T(128)S(1)}, u32[]{:S(2)}) copy-start(f32[128]{0:T(128)S(1)} %negate_multiply_fusion.1) | copy-start | bytes 1540
  365.7 154.2 %reduce-scatter.8.cloned.1.call-start = ((), (), s32[]{:S(2)}) async-start(), calls=%async_computation.9 | async-start | bytes 3932160 | tf_op jit(solution)/shard_map/reduce_scatter | solution.py:41
  479.9 72.9 %reduce-scatter.10.cloned.1.call-start = ((), (), s32[]{:S(2)}) async-start(), calls=%async_computation.10 | async-start | bytes 1179648 | tf_op jit(solution)/shard_map/reduce_scatter | solution.py:41
  520.0 62.1 %reduce-scatter.14.cloned.1.call-start = ((), (), s32[]{:S(2)}) async-start(), calls=%async_computation.12 | async-start | bytes 7151616 | tf_op jit(solution)/shard_map/reduce_scatter | solution.py:58
  524.9 77.8 %reduce-scatter.12.cloned.1.call-start = ((), (), s32[]{:S(2)}) async-start(), calls=%async_computation.11 | async-start | bytes 14450688 | tf_op jit(solution)/shard_map/reduce_scatter | solution.py:58
  552.8 5.0 copy-start.3
  557.8 6.8 copy-start.14
  582.0 395.2 %all-reduce.8.cloned.1.call-start = ((), (), s32[]{:S(2)}) async-start(), calls=%async_computation.13 | async-start | bytes 28311552 | tf_op jit(solution)/shard_map/psum | solution.py:254
  611.9 5.2 copy-start.9
  612.0 5.2 copy-start.22
  612.0 7.7 copy-start.4
  977.2 6.2 copy-start.13
  977.2 7.2 copy-start.12
  977.2 10.3 %slice-start = ((s8[4718592]{0:T(1024)(128)(4,1)}), s8[524288]{0:T(1024)(128)(4,1)S(1)}, s32[]{:S(2)}) async-start(s8[4718592]{0:T(1024)(128)(4,1)} %bitcast.92), calls=%async_computation.14 | async-start | bytes 1048576
  (14 other events, 28.9 us)
Sparse Core Ops, SparseCore 0:
  20.7 27.1 all-gather.6
  50.1 19.6 all-gather.10
  73.1 136.2 all-gather.8
  365.8 113.9 reduce-scatter.5
  482.1 37.7 reduce-scatter.7
  522.1 21.2 reduce-scatter.9
  546.0 14.6 reduce-scatter.13
  582.2 20.4 reduce-scatter.11
  612.1 200.2 all-reduce.7
where the time goes:
time: 1010 us; the launch traced here: 997 us
  blocking collectives  359 us (36%)
  waiting for transfers between devices  337 us (33%)
  matrix products  118 us (12%)
  local copies, waits for them, and re-layouts  110 us (11%)
  other arithmetic  56.7 us (6%)
  between operations  16 us (2%)
    psum x1, blocking collectives, local(): lax.psum((shares[0], shares[1], shares[2], shares[3], shares[4], shares[5...  351 us
    reduce_scatter x3, waiting for transfers between devices, sum_in_order(): blocks = lax.psum_scatter(blocks, axes[k], scatter_dimension=0, tiled=True)  154 us
    all_gather x1, waiting for transfers between devices, sent_together_2(): whole, at, outs = (lax.all_gather(both, axis, axis=dim, tiled=True), 0, [])  136 us
    concatenate x4, local copies, waits for them, and re-layouts, local(): jnp.concatenate([grad_keys.reshape(count, width), grad_values.reshape(cou...  43.4 us
    all_gather x2, waiting for transfers between devices, sent_together(): whole = lax.all_gather(both, axis, axis=dim, tiled=True)  30.6 us
  transfers between devices with their start and end apart: 9, of which 6 were waited for; matrix products, arithmetic and copies ran while one was open for 9% of the time, Pallas kernels for 0%

commit v1 on v0

v1 whole, which is shorter than its diff:
```python
import functools
import math

import jax
import jax.numpy as jnp
from jax import lax
from jax.experimental import pallas as pl
from jax.experimental.pallas import tpu as pltpu
from jax.sharding import Mesh
from jax.sharding import PartitionSpec as P

H = 12
HD = 64
D = 768
CTX = ("ctx_0", "ctx_1", "ctx_2")
f32 = jnp.float32
bf16 = jnp.bfloat16
MESH = pl.DeviceIdType.MESH
ANY = pl.ANY
MIB = 1024 * 1024


def place(axis):
    if axis == "x":
        return lax.axis_index("ctx_2")
    if axis == "z":
        return lax.axis_index("ctx_1")
    return lax.axis_index("ctx_0") * 2 + lax.axis_index("seq")


def away(axis, step):
    at = lax.rem(place(axis) + step + 4, 4)
    if axis == "x":
        return {"ctx_2": at}
    if axis == "z":
        return {"ctx_1": at}
    return {"ctx_0": at // 2, "seq": lax.rem(at, 2)}


def sibling():
    return {"wsh": 1 - lax.axis_index("wsh")}


def far():
    return {"ctx_0": 1 - lax.axis_index("ctx_0")}


def meet(devices):
    barrier = pltpu.get_barrier_semaphore()
    for d in devices:
        pl.semaphore_signal(barrier, inc=1, device_id=d, device_id_type=MESH)
    pl.semaphore_wait(barrier, len(devices))


class Sends:
    def __init__(self, send, recv):
        self.send, self.recv, self.used, self.all = send, recv, 0, []

    def start(self, src, dst, device):
        k = self.used
        self.used += 1
        copy = pltpu.make_async_remote_copy(
            src_ref=src,
            dst_ref=dst,
            send_sem=self.send.at[k],
            recv_sem=self.recv.at[k],
            device_id=device,
            device_id_type=MESH,
        )
        copy.start()
        self.all.append(copy)
        return copy

    def finish(self):
        for copy in self.all:
            copy.wait_send()


def gather_kernel(rows, n_pair, *refs):
    n = len(rows)
    ins, pair_ins = refs[:n], refs[n : n + n_pair]
    outs, pair_outs = refs[n + n_pair : 2 * n + n_pair], refs[2 * n + n_pair : 2 * (n + n_pair)]
    send, recv, local = refs[2 * (n + n_pair) :]
    sends = Sends(send, recv)
    y, z, x = (lax.axis_index(a) for a in CTX)
    core = lax.axis_index("wsh")
    devices = [away("x", 1), away("x", -1), away("z", 1), away("z", -1), far()]
    if n_pair:
        devices.append(sibling())
    meet(devices)
    locals_ = []

    def keep(src, dst):
        copy = pltpu.make_async_copy(src, dst, local.at[len(locals_)])
        copy.start()
        locals_.append(copy)
        return copy

    own = [keep(i, o.at[y, z, x]) for i, o in zip(ins, outs)]
    crossing = [sends.start(i, o.at[y, z, x], far()) for i, o in zip(ins, outs)]

    def first(layer, mine):
        flights = []
        for i, o, r in zip(ins, outs, rows):
            h = r // 2
            for axis, lo in (("x", 0), ("z", h)):
                src = i.at[pl.ds(lo, h)] if mine else o.at[layer, z, x, pl.ds(lo, h)]
                dst = o.at[layer, z, x, pl.ds(lo, h)]
                flights.append(
                    [sends.start(src, dst, away(axis, 1)), sends.start(src, dst, away(axis, -1))]
                )
        return flights

    def first_on(layer, flights):
        later, at = [], 0
        for o, r in zip(outs, rows):
            q = r // 4
            for axis, lo in (("x", 0), ("z", 2 * q)):
                right, left = flights[at]
                at += 1
                pos = place(axis)
                before, after = lax.rem(pos + 3, 4), lax.rem(pos + 1, 4)
                right.wait_recv()
                if axis == "x":
                    a = o.at[layer, z, before, pl.ds(lo, q)]
                    b = o.at[layer, z, after, pl.ds(lo + q, q)]
                else:
                    a = o.at[layer, before, x, pl.ds(lo, q)]
                    b = o.at[layer, after, x, pl.ds(lo + q, q)]
                up = sends.start(a, a, away(axis, 1))
                left.wait_recv()
                later.append([up, sends.start(b, b, away(axis, -1))])
        return later

    def second(layer, flights):
        later, at = [], 0
        for o, r in zip(outs, rows):
            h = r // 2
            for axis, lo in (("z", 0), ("x", h)):
                for copy in flights[at]:
                    copy.wait_recv()
                at += 1
                if axis == "z":
                    a = o.at[layer, z, :, pl.ds(lo, h)]
                else:
                    a = o.at[layer, :, x, pl.ds(lo, h)]
                later.append([sends.start(a, a, away(axis, 1)), sends.start(a, a, away(axis, -1))])
        return later

    def second_on(layer, flights):
        later, at = [], 0
        for o, r in zip(outs, rows):
            h = r // 2
            for axis, lo in (("z", 0), ("x", h)):
                right, left = flights[at]
                at += 1
                pos = place(axis)
                before, after = lax.rem(pos + 3, 4), lax.rem(pos + 1, 4)
                right.wait_recv()
                if axis == "z":
                    a = o.at[layer, before, pl.ds(0, 2), pl.ds(lo, h)]
                    b = o.at[layer, after, pl.ds(2, 2), pl.ds(lo, h)]
                else:
                    a = o.at[layer, pl.ds(0, 2), before, pl.ds(lo, h)]
                    b = o.at[layer, pl.ds(2, 2), after, pl.ds(lo, h)]
                up = sends.start(a, a, away(axis, 1))
                left.wait_recv()
                later.append([up, sends.start(b, b, away(axis, -1))])
        return later

    mine = first(y, True)
    pairs = []
    for i, o in zip(pair_ins, pair_outs):
        pairs.append(sends.start(i, o.at[core], sibling()))
        keep(i, o.at[core])
    other = 1 - y
    mine = first_on(y, mine)
    for copy in crossing:
        copy.wait_recv()
    theirs = first(other, False)
    for copy in own:
        copy.wait()
    mine = second(y, mine)
    theirs = first_on(other, theirs)
    mine = second_on(y, mine)
    theirs = second(other, theirs)
    theirs = second_on(other, theirs)
    for flights in (mine, theirs):
        for pair in flights:
            for copy in pair:
                copy.wait_recv()
    for copy in pairs:
        copy.wait_recv()
    for copy in locals_[len(own) :]:
        copy.wait()
    sends.finish()


def gather(arrays, pairs, cid):
    n, m = len(arrays), len(pairs)
    outs = pl.pallas_call(
        functools.partial(gather_kernel, tuple(a.shape[0] for a in arrays), m),
        out_shape=[jax.ShapeDtypeStruct((2, 4, 4, *a.shape), a.dtype) for a in arrays]
        + [jax.ShapeDtypeStruct((2, *a.shape), a.dtype) for a in pairs],
        in_specs=[pl.BlockSpec(memory_space=ANY)] * (n + m),
        out_specs=[pl.BlockSpec(memory_space=ANY)] * (n + m),
        scratch_shapes=[
            pltpu.SemaphoreType.DMA((33 * n + m,)),
            pltpu.SemaphoreType.DMA((33 * n + m,)),
            pltpu.SemaphoreType.DMA((n + m,)),
        ],
        compiler_params=pltpu.CompilerParams(collective_id=cid, has_side_effects=True),
    )(*arrays, *pairs)
    return outs[:n], outs[n:]


ORDERS = (("x", "y", "z"), ("y", "z", "x"), ("z", "x", "y"))
AXES = ("x", "y", "z")
SPLIT = ((192, 192), (48, 48), (32, 16))
CHUNK = ((384, 768), (96, 768), (48, 384))


def reduce_kernel(
    g0, g1, g2, small, out, small_out,
    acc, pair, t0, t1, t2, u0, u1, u2, cur, slots, send, recv, local,
):
    core = lax.axis_index("wsh")
    twin = 1 - core
    sends = Sends(send, recv)
    tt, uu = (t0, t1, t2), (u0, u1, u2)
    pos = {a: place(a) for a in AXES}
    meet([sibling()] + [away(a, k) for a in AXES for k in (1, 2, 3)])

    def share(s, m, half):
        if s == 0:
            return g0.at[m, pl.ds(pl.multiple_of(half * 384, 384), 384)]
        if s == 1:
            return g1.at[pl.ds(pl.multiple_of(half * 384, 384), 384), pl.ds(m * 768, 768)]
        return g2.at[pl.ds(pl.multiple_of(half * 1536 + m * 384, 384), 384)]

    small_pair = sends.start(small.at[twin], slots.at[3, 0], sibling())
    flights, kept = [], []
    for m in range(4):
        for s in range(3):
            flights.append((s, m, sends.start(share(s, m, twin), pair.at[s, m], sibling())))
            copy = pltpu.make_async_copy(share(s, m, core), acc.at[s, m], local.at[s * 4 + m])
            copy.start()
            kept.append(copy)
    mine = pltpu.make_async_copy(small.at[core], cur, local.at[12])
    mine.start()
    mine.wait()
    small_pair.wait_recv()
    cur[...] = cur[...] + slots[3, 0]

    def add(dst, dst_at, src, src_at, shape):
        rows, cols = shape

        @pl.loop(0, rows // 16)
        def _(k):
            a = dst_at(pl.multiple_of(k * 16, 16))
            b = src_at(pl.multiple_of(k * 16, 16))
            dst[a] = (dst[a].astype(f32) + src[b].astype(f32)).astype(bf16)

    for (s, m, flight), copy in zip(flights, kept):
        copy.wait()
        flight.wait_recv()
        add(
            acc, lambda r, s=s, m=m: (s, m, pl.ds(r, 16)),
            pair, lambda r, s=s, m=m: (s, m, pl.ds(r, 16)), (384, 768),
        )

    def region(ph, s, c, r, n):
        a, b, _ = (pos[k] for k in ORDERS[s])
        if ph == 0:
            return (s, c, pl.ds(r, n))
        if ph == 1:
            return (s, a, pl.ds(pl.multiple_of(96 * c + r, 16), n))
        return (
            s, a, pl.ds(pl.multiple_of(96 * b + 48 * (c // 2) + r, 16), n),
            pl.ds(pl.multiple_of(lax.rem(c, 2) * 384, 384), 384),
        )

    small_axis = {}
    for ph in range(3):
        axis = AXES[ph]
        slots[ph, pos[axis]] = cur[...]
        small_axis = [
            sends.start(cur, slots.at[ph, pos[axis]], away(axis, k)) for k in (1, 2, 3)
        ]
        rows, cols = CHUNK[ph]
        near, rest = SPLIT[ph]
        steps = []
        for s in range(3):
            axis_s = ORDERS[s][ph]
            p = pos[axis_s]
            c = lax.rem(p + 2, 4)
            steps.append((
                sends.start(
                    acc.at[region(ph, s, c, 0, near)], tt[ph].at[s, 0, pl.ds(0, near)], away(axis_s, 1)
                ),
                sends.start(
                    acc.at[region(ph, s, c, near, rest)], tt[ph].at[s, 1, pl.ds(0, rest)], away(axis_s, -1)
                ),
            ))
        nexts = []
        for s in range(3):
            axis_s = ORDERS[s][ph]
            p = pos[axis_s]
            up, down = lax.rem(p + 1, 4), lax.rem(p + 3, 4)
            steps[s][0].wait_recv()
            add(
                acc, lambda r, s=s, up=up: region(ph, s, up, r, 16),
                tt[ph], lambda r, s=s: (s, 0, pl.ds(r, 16)), (near, cols),
            )
            a = sends.start(acc.at[region(ph, s, up, 0, rows)], uu[ph].at[s, 0], away(axis_s, 1))
            steps[s][1].wait_recv()
            add(
                acc, lambda r, s=s, down=down: region(ph, s, down, near + r, 16),
                tt[ph], lambda r, s=s: (s, 1, pl.ds(r, 16)), (rest, cols),
            )
            b = sends.start(acc.at[region(ph, s, down, 0, rows)], uu[ph].at[s, 1], away(axis_s, -1))
            nexts.append((a, b))
        for s in range(3):
            p = pos[ORDERS[s][ph]]
            for k in range(2):
                nexts[s][k].wait_recv()
                add(
                    acc, lambda r, s=s, p=p: region(ph, s, p, r, 16),
                    uu[ph], lambda r, s=s, k=k: (s, k, pl.ds(r, 16)), (rows, cols),
                )
        for copy in small_axis:
            copy.wait()
        sends.all = [c for c in sends.all if all(c is not d for d in small_axis)]
        cur[...] = (slots[ph, 0] + slots[ph, 1]) + (slots[ph, 2] + slots[ph, 3])

    small_out[...] = cur[...]

    for ph in (2, 1, 0):
        rows, cols = CHUNK[ph]
        near, rest = SPLIT[ph]
        steps = []
        for s in range(3):
            axis_s = ORDERS[s][ph]
            p = pos[axis_s]
            here = region(ph, s, p, 0, rows)
            if ph == 2:
                kept_copy = pltpu.make_async_copy(acc.at[here], out.at[here], local.at[s])
                kept_copy.start()
                src = acc.at[here]
            else:
                kept_copy = None
                src = out.at[here]
            steps.append((
                sends.start(src, out.at[here], away(axis_s, 1)),
                sends.start(src, out.at[here], away(axis_s, -1)),
                kept_copy,
            ))
        nexts = []
        for s in range(3):
            axis_s = ORDERS[s][ph]
            p = pos[axis_s]
            up, down = lax.rem(p + 1, 4), lax.rem(p + 3, 4)
            steps[s][0].wait_recv()
            part = out.at[region(ph, s, down, 0, near)]
            a = sends.start(part, part, away(axis_s, 1))
            steps[s][1].wait_recv()
            part = out.at[region(ph, s, up, near, rest)]
            b = sends.start(part, part, away(axis_s, -1))
            nexts.append((a, b))
        for s in range(3):
            if steps[s][2] is not None:
                steps[s][2].wait()
            for copy in nexts[s]:
                copy.wait_recv()
    sends.finish()


def reduce_params(g0, g1, g2, small, cid):
    scratch = [pltpu.VMEM((3, 4, 384, 768), bf16), pltpu.VMEM((3, 4, 384, 768), bf16)]
    scratch += [pltpu.VMEM((3, 2, SPLIT[k][0], CHUNK[k][1]), bf16) for k in range(3)]
    scratch += [pltpu.VMEM((3, 2, *CHUNK[k]), bf16) for k in range(3)]
    scratch += [pltpu.VMEM((40, 128), f32), pltpu.VMEM((4, 4, 40, 128), f32)]
    count = 1 + 12 + 9 + 3 * 24
    scratch += [
        pltpu.SemaphoreType.DMA((count,)),
        pltpu.SemaphoreType.DMA((count,)),
        pltpu.SemaphoreType.DMA((13,)),
    ]
    return pl.pallas_call(
        reduce_kernel,
        out_shape=[
            jax.ShapeDtypeStruct((3, 4, 384, 768), bf16),
            jax.ShapeDtypeStruct((40, 128), f32),
        ],
        in_specs=[pl.BlockSpec(memory_space=ANY)] * 4,
        out_specs=[pl.BlockSpec(memory_space=ANY), pl.BlockSpec(memory_space=pltpu.VMEM)],
        scratch_shapes=scratch,
        compiler_params=pltpu.CompilerParams(
            collective_id=cid, has_side_effects=True, vmem_limit_bytes=40 * MIB
        ),
    )(g0, g1, g2, small)


def nt(a, b):
    return lax.dot_general(a, b, (((1,), (1,)), ((), ())), preferred_element_type=f32)


def nn(a, b):
    return jnp.dot(a, b, preferred_element_type=f32)


def stacked(block):
    lane = lax.broadcasted_iota(jnp.int32, block.shape, 1) // HD
    zero = jnp.zeros_like(block)
    return jnp.concatenate([jnp.where(lane == i, block, zero) for i in range(4)], axis=0)


def unstacked(tall):
    n = tall.shape[0] // 4
    lane = lax.broadcasted_iota(jnp.int32, (n, tall.shape[1]), 1) // HD
    total = jnp.where(lane == 0, tall[:n], 0.0)
    for i in range(1, 4):
        total = total + jnp.where(lane == i, tall[i * n : (i + 1) * n], 0.0)
    return total


def as_rows(column):
    wide = jnp.broadcast_to(column, (column.shape[0], 128))
    return jnp.concatenate(
        [wide[i * 128 : (i + 1) * 128].T[:1] for i in range(4)] + [jnp.zeros((4, 128), f32)], axis=0
    )


TILE = 1024


def forward_kernel(q_ref, k_ref, v_ref, bias_ref, attn_ref, lse_ref, rows_ref, score):
    q = stacked(q_ref[...] * jnp.asarray(0.125, bf16))
    top = None
    for t in range(4096 // TILE):
        at = pl.ds(t * TILE, TILE)
        s = nt(q, k_ref[at, :]) + bias_ref[:, at]
        score[:, at] = s
        m = jnp.max(s, axis=-1, keepdims=True)
        top = m if top is None else jnp.maximum(top, m)
    total, out = 0.0, 0.0
    for t in range(4096 // TILE):
        at = pl.ds(t * TILE, TILE)
        p = jnp.exp(score[:, at] - top)
        total = total + jnp.sum(p, axis=-1, keepdims=True)
        out = out + nn(p.astype(bf16), v_ref[at, :])
    attn_ref[...] = unstacked(out * (1.0 / total))
    lse = top + jnp.log(total)
    lse_ref[0] = jnp.broadcast_to(lse, (512, 128))
    rows_ref[0] = as_rows(lse)


def attend(q, k, v, bias):
    wide = pl.BlockSpec((4096, 256), lambda g: (0, g))
    own = pl.BlockSpec((128, 256), lambda g: (0, g))
    return pl.pallas_call(
        forward_kernel,
        grid=(3,),
        out_shape=[
            jax.ShapeDtypeStruct((128, D), f32),
            jax.ShapeDtypeStruct((3, 512, 128), f32),
            jax.ShapeDtypeStruct((3, 8, 128), f32),
        ],
        in_specs=[own, wide, wide, pl.BlockSpec((1, 4096), lambda g: (0, 0))],
        out_specs=[
            own,
            pl.BlockSpec((1, 512, 128), lambda g: (g, 0, 0)),
            pl.BlockSpec((1, 8, 128), lambda g: (g, 0, 0)),
        ],
        scratch_shapes=[pltpu.VMEM((512, 4096), f32)],
        compiler_params=pltpu.CompilerParams(vmem_limit_bytes=56 * MIB),
    )(q, k, v, bias)


def query_kernel(q_ref, k_ref, v_ref, bias_ref, g_ref, attn_ref, lse_ref, dq_ref, rows_ref):
    q = stacked(q_ref[...] * jnp.asarray(0.125, bf16))
    g = stacked(g_ref[...])
    attn = attn_ref[...]
    tall = jnp.concatenate([attn] * 4, axis=0)
    delta = jnp.sum(g.astype(f32) * tall, axis=-1, keepdims=True)
    rows_ref[0] = as_rows(delta)
    lse = lse_ref[0][:, :1]
    dq = 0.0
    for t in range(4096 // TILE):
        at = pl.ds(t * TILE, TILE)
        p = jnp.exp(nt(q, k_ref[at, :]) + bias_ref[:, at] - lse)
        dp = nt(g, v_ref[at, :])
        ds = (p * (dp - delta)).astype(bf16)
        dq = dq + nn(ds, k_ref[at, :])
    dq_ref[...] = (unstacked(dq) * 0.125).astype(bf16)


def query_grads(q, k, v, bias, g, attn, lse):
    wide = pl.BlockSpec((4096, 256), lambda g: (0, g))
    own = pl.BlockSpec((128, 256), lambda g: (0, g))
    return pl.pallas_call(
        query_kernel,
        grid=(3,),
        out_shape=[jax.ShapeDtypeStruct((128, D), bf16), jax.ShapeDtypeStruct((3, 8, 128), f32)],
        in_specs=[
            own, wide, wide, pl.BlockSpec((1, 4096), lambda g: (0, 0)), own, own,
            pl.BlockSpec((1, 512, 128), lambda g: (g, 0, 0)),
        ],
        out_specs=[own, pl.BlockSpec((1, 8, 128), lambda g: (g, 0, 0))],
        compiler_params=pltpu.CompilerParams(vmem_limit_bytes=56 * MIB),
    )(q, k, v, bias, g, attn, lse)


def key_kernel(k_ref, v_ref, bias_ref, q_ref, g_ref, lse_ref, delta_ref, dk_ref, dv_ref):
    k = stacked(k_ref[...] * jnp.asarray(0.125, bf16))
    v = stacked(v_ref[...])
    bias = jnp.concatenate([bias_ref[:, :1]] * 4, axis=0)
    dk, dv = 0.0, 0.0
    for t in range(4096 // TILE):
        at = pl.ds(t * TILE, TILE)
        q, g = q_ref[at, :], g_ref[at, :]
        lse = jnp.concatenate(
            [jnp.broadcast_to(lse_ref[0, i : i + 1, at], (128, TILE)) for i in range(4)], axis=0
        )
        delta = jnp.concatenate(
            [jnp.broadcast_to(delta_ref[0, i : i + 1, at], (128, TILE)) for i in range(4)], axis=0
        )
        p = jnp.exp(nt(k, q) + bias - lse)
        ds = (p * (nt(v, g) - delta)).astype(bf16)
        dv = dv + nn(p.astype(bf16), g)
        dk = dk + nn(ds, q)
    dk_ref[...] = (unstacked(dk) * 0.125).astype(bf16)
    dv_ref[...] = unstacked(dv).astype(bf16)


def key_grads(k, v, bias, q, g, lse, delta):
    wide = pl.BlockSpec((4096, 256), lambda g: (0, g))
    own = pl.BlockSpec((128, 256), lambda g: (0, g))
    stat = pl.BlockSpec((1, 8, 4096), lambda g: (g, 0, 0))
    return pl.pallas_call(
        key_kernel,
        grid=(3,),
        out_shape=[jax.ShapeDtypeStruct((128, D), bf16)] * 2,
        in_specs=[own, own, pl.BlockSpec((128, 128), lambda g: (0, 0)), wide, wide, stat, stat],
        out_specs=[own, own],
        compiler_params=pltpu.CompilerParams(vmem_limit_bytes=56 * MIB),
    )(k, v, bias, q, g, lse, delta)


def layer_norm(resid, gain, shift):
    centre = resid - jnp.mean(resid, axis=-1, keepdims=True)
    spread = jnp.mean(centre * centre, axis=-1, keepdims=True)
    return centre * lax.rsqrt(spread + 1e-12) * gain + shift


def gelu_exact(value):
    return jax.nn.gelu(value, approximate=False)


def local(
    tokens, lengths, w_query, b_query, w_key, w_value, b_value, w_out, b_out, gain_one, shift_one,
    w_up, b_up, w_down, b_down, gain_two, shift_two, cotangent,
):
    inputs = tokens[0]
    vectors = jnp.stack(
        [b_query, b_value, b_out, gain_one, shift_one, b_down, gain_two, shift_two]
    )
    vectors = jnp.concatenate([vectors, b_up.reshape(4, 384), jnp.zeros((4, 384), bf16)], axis=0)
    (xs,), whole = gather(
        [inputs], [w_query, w_key, w_value, w_out, w_up, w_down, vectors], 0
    )
    wq, wk, wv, wo, wup, wdown = (w.reshape(-1, w.shape[-1]) for w in whole[:6])
    vecs = whole[6].astype(f32)
    bq, bv, bo, gone, sone, bdown, gtwo, stwo = (
        vecs[:, i].reshape(768) for i in range(8)
    )
    bup = vecs[:, 8:12].reshape(3072)
    xs = xs.reshape(4096, D)
    seq_len = lengths[0]
    block = (lax.axis_index("ctx_0") * 4 + lax.axis_index("ctx_1")) * 4 + lax.axis_index("ctx_2")
    all_q = (jnp.dot(xs, wq, preferred_element_type=f32) + bq).astype(bf16)
    all_k = jnp.dot(xs, wk, preferred_element_type=f32).astype(bf16)
    all_v = (jnp.dot(xs, wv, preferred_element_type=f32) + bv).astype(bf16)
    q = lax.dynamic_slice_in_dim(all_q, block * 128, 128)
    k = lax.dynamic_slice_in_dim(all_k, block * 128, 128)
    v = lax.dynamic_slice_in_dim(all_v, block * 128, 128)
    bias = jnp.where(jnp.arange(4096) < seq_len, 0.0, -1e30).astype(f32)[None]
    own_bias = jnp.where(jnp.arange(128) + block * 128 < seq_len, 0.0, -1e30).astype(f32)
    own_bias = jnp.broadcast_to(own_bias[:, None], (128, 128))
    attn, lse, lse_rows = attend(q, all_k, all_v, bias)
    mixed = attn.astype(bf16)
    resid_one = inputs.astype(f32) + jnp.dot(mixed, wo, preferred_element_type=f32) + bo
    first, pull_one = jax.vjp(layer_norm, resid_one, gone, sone)
    first_low = first.astype(bf16)
    pre = jnp.dot(first_low, wup, preferred_element_type=f32) + bup
    act, pull_gelu = jax.vjp(gelu_exact, pre)
    act_low = act.astype(bf16)
    resid_two = first + jnp.dot(act_low, wdown, preferred_element_type=f32) + bdown
    result, pull_two = jax.vjp(layer_norm, resid_two, gtwo, stwo)
    grad_resid_two, grad_gtwo, grad_stwo = pull_two(cotangent[0].astype(f32))
    grad_down_low = grad_resid_two.astype(bf16)
    grad_bdown = jnp.sum(grad_resid_two, axis=0)
    grad_wdown = jnp.einsum("tf,td->fd", act_low, grad_down_low, preferred_element_type=f32)
    grad_act = jnp.einsum("td,fd->tf", grad_down_low, wdown, preferred_element_type=f32)
    grad_pre_low = pull_gelu(grad_act)[0].astype(bf16)
    grad_bup = jnp.sum(grad_pre_low.astype(f32), axis=0)
    grad_wup = jnp.einsum("td,tf->df", first_low, grad_pre_low, preferred_element_type=f32)
    grad_first = grad_resid_two + jnp.einsum(
        "tf,df->td", grad_pre_low, wup, preferred_element_type=f32
    )
    grad_resid_one, grad_gone, grad_sone = pull_one(grad_first)
    grad_branch = grad_resid_one.astype(bf16)
    grad_bout = jnp.sum(grad_resid_one, axis=0)
    grad_mixed = jnp.einsum("te,de->td", grad_branch, wo, preferred_element_type=f32).astype(bf16)
    grad_query_low, delta_rows = query_grads(q, all_k, all_v, bias, grad_mixed, attn, lse)
    pad = jnp.zeros((4, 128), f32)
    stats = jnp.concatenate(
        [lse_rows[:, :4].reshape(12, 128), pad, delta_rows[:, :4].reshape(12, 128), pad], axis=0
    )
    (all_g, all_stats), _ = gather([grad_mixed, stats], [], 1)
    all_g = all_g.reshape(4096, D)
    all_stats = all_stats.reshape(32, 32, 128).transpose(1, 0, 2).reshape(32, 4096)
    all_lse = jnp.pad(all_stats[:12].reshape(3, 4, 4096), ((0, 0), (0, 4), (0, 0)))
    all_delta = jnp.pad(all_stats[16:28].reshape(3, 4, 4096), ((0, 0), (0, 4), (0, 0)))
    grad_keys_low, grad_values_low = key_grads(k, v, own_bias, all_q, all_g, all_lse, all_delta)
    lefts = jnp.stack([inputs, inputs, inputs, mixed])
    rights = jnp.stack([grad_query_low, grad_keys_low, grad_values_low, grad_branch])
    grad_four = jnp.einsum("ktd,kte->kde", lefts, rights, preferred_element_type=f32).astype(bf16)
    grad_bq = jnp.sum(grad_query_low.astype(f32), axis=0)
    grad_bv = jnp.sum(grad_values_low.astype(f32), axis=0)
    grad_inputs = grad_resid_one + jnp.einsum(
        "te,de->td", grad_query_low, wq, preferred_element_type=f32
    )
    grad_inputs = grad_inputs + jnp.einsum(
        "te,de->td", grad_keys_low, wk, preferred_element_type=f32
    )
    grad_inputs = grad_inputs + jnp.einsum(
        "te,de->td", grad_values_low, wv, preferred_element_type=f32
    )
    small = jnp.stack(
        [grad_bq, grad_bv, grad_bout, grad_gone, grad_sone, grad_bdown, grad_gtwo, grad_stwo]
    )
    small = small.reshape(8, 2, 384).transpose(1, 0, 2).reshape(2, 3072)
    small = jnp.concatenate(
        [small, grad_bup.reshape(2, 1536), jnp.zeros((2, 512), f32)], axis=1
    ).reshape(2, 40, 128)
    big, small = reduce_params(
        grad_four, grad_wup.astype(bf16), grad_wdown.astype(bf16), small, 2
    )
    small = small.reshape(5120)
    tot_bq, tot_bv, tot_bo, tot_gone, tot_sone, tot_bdown, tot_gtwo, tot_stwo = (
        small[i * 384 : (i + 1) * 384] for i in range(8)
    )
    tot_bup = small[3072:4608]
    big = big.astype(f32)
    return (
        result.astype(bf16)[None],
        grad_inputs[None],
        big[0, 0],
        tot_bq,
        big[0, 1],
        big[0, 2],
        tot_bv,
        big[0, 3],
        tot_bo,
        tot_gone,
        tot_sone,
        big[1].transpose(1, 0, 2).reshape(384, 3072),
        tot_bup,
        big[2].reshape(1536, 768),
        tot_bdown,
        tot_gtwo,
        tot_stwo,
    )


def solution(mesh):
    split = Mesh(
        mesh.devices.reshape(mesh.shape["seq"], 2, 4, 4, mesh.shape["wsh"]),
        ("seq", "ctx_0", "ctx_1", "ctx_2", "wsh"),
    )
    rows = P(("seq", "wsh"), CTX, None)
    mat, vec = P("wsh", None), P("wsh")
    params = (mat, vec, mat, mat, vec, mat, vec, vec, vec, mat, vec, mat, vec, vec, vec)
    return jax.shard_map(
        local,
        mesh=split,
        in_specs=(rows, P(("seq", "wsh")), *params, rows),
        out_specs=(rows, rows, *params),
        check_vma=False,
    )
```

time: 1010 us -> 569 us (0.56)
  Pallas kernels: 0 us -> 425 us
  blocking collectives: 359 us -> 0 us
  waiting for transfers between devices: 337 us -> 0 us
  local copies, waits for them, and re-layouts: 110 us -> 49.8 us
  matrix products: 118 us -> 69.1 us
  other arithmetic: 56.7 us -> 13.6 us
  between operations: 16 us -> 2.26 us
    pallas_call x0 -> x6, Pallas kernels: none -> 425 us  [the longest x2 274 us: gather(): pl.pallas_call(functools.partial(gather_kernel, tuple((a.shape[0] for a i...]
    psum x1 -> x0, blocking collectives: 351 us -> none  [local(): lax.psum((shares[0], shares[1], shares[2], shares[3], shares[4], shares[5...]
    reduce_scatter x5 -> x0, waiting for transfers between devices: 170 us -> none  [the longest x3 154 us: sum_in_order(): blocks = lax.psum_scatter(blocks, axes[k], scatter_dimension=0, tiled=True)]
    all_gather x3 -> x0, waiting for transfers between devices: 167 us -> none  [the longest x1 136 us: sent_together_2(): whole, at, outs = (lax.all_gather(both, axis, axis=dim, tiled=True), 0, [])]
    concatenate x6 -> x2, local copies, waits for them, and re-layouts: 70.2 us -> 1.25 us  [the longest x1 1.24 us: local(): jnp.concatenate([vectors, b_up.reshape(4, 384), jnp.zeros((4, 384), bf16)...]
    dot_general x14 -> x5, matrix products: 94.7 us -> 41 us  [the longest x1 9.82 us: local(): all_k = jnp.dot(xs, wk, preferred_element_type=f32).astype(bf16)]
    concatenate x4 -> x1, other arithmetic: 19.9 us -> 0.61 us  [local(): jnp.concatenate([lse_rows[:, :4].reshape(12, 128), pad, delta_rows[:, :4]...]
    reduce_sum x2 -> x1, other arithmetic: 12.9 us -> 0.04 us  [local(): grad_bq = jnp.sum(grad_query_low.astype(f32), axis=0)]
  transfers between devices with their start and end apart: 9 -> 0, of which waited for: 6 -> 0; matrix products, arithmetic and copies ran while one was open for 9% -> 0% of each run, Pallas kernels for 0% -> 0%
where the time goes in v1:
time: 569 us; the launch traced here: 559 us
  Pallas kernels  425 us (75%)
  matrix products  69.1 us (12%)
  local copies, waits for them, and re-layouts  49.8 us (9%)
  other arithmetic  13.6 us (2%)
    pallas_call x2, Pallas kernels, gather(): pl.pallas_call(functools.partial(gather_kernel, tuple((a.shape[0] for a i...  274 us
    pallas_call x1, Pallas kernels, reduce_params(): pl.pallas_call(reduce_kernel, out_shape=[jax.ShapeDtypeStruct((3, 4, 384,...  96 us
    pallas_call x1, Pallas kernels, attend(): pl.pallas_call(forward_kernel, grid=(3,), out_shape=[jax.ShapeDtypeStruct...  21 us
    pallas_call x1, Pallas kernels, key_grads(): pl.pallas_call(key_kernel, grid=(3,), out_shape=[jax.ShapeDtypeStruct((12...  18 us
    pallas_call x1, Pallas kernels, query_grads(): pl.pallas_call(query_kernel, grid=(3,), out_shape=[jax.ShapeDtypeStruct((...  16.1 us
    unnamed x61, local copies, waits for them, and re-layouts  13.2 us

profile of v1, /device:TPU:0, one launch (start us, length us, event | category | flops | bytes accessed | tf_op | source)
XLA Modules:
  0.0 559.4 jit_solution(1529331600532016411)
XLA Ops:
  8.1 226.8 %shard_map.305 = (bf16[2,4,4,128,768]{4,3,2,1,0:T(8,128)(2,1)}, bf16[2,384,768]{2,1,0:T(8,128)(2,1)}, bf16[2,384,768]{2,1,0:T(8,128)(2,1)}, bf16[2,384,768]{2,1,...) custom-call(bf16[128,768]{1,0:T(8,128)(2,1)} %bitcast.126, ...), custom_call_target="tpu_custom_call" | custom-call | tf_op jit(solution)/shard_map/pallas_call | solution.py:201
  236.5 9.3 %add_convert_fusion.1.q_ref = bf16[4096,768]{1,0:T(8,128)(2,1)} fusion(f32[768]{0:T(1024)S(1)} %add.133, bf16[4096,768]{1,0:T(8,128)(2,1)} %bitcast.131, bf16[768,768]{1,0:T(8,128)(2,1)} %bitcast.122), kind=kOutput, calls=%fused_computation.1 | convolution fusion | flops 4838129664 | bytes 13765632 | tf_op jit(solution)/shard_map/dot_general | solution.py:581
  245.8 1.6 constant_dynamic-slice_fusion.2.q_ref
  247.4 9.8 %convolution_convert_fusion.k_ref = bf16[4096,768]{1,0:T(8,128)(2,1)} fusion(bf16[4096,768]{1,0:T(8,128)(2,1)} %bitcast.132, bf16[768,768]{1,0:T(8,128)(2,1)S(1)} %bitcast.120), kind=kOutput, calls=%fused_computation.2 | convolution fusion | flops 4834983936 | bytes 13762560 | tf_op jit(solution)/shard_map/dot_general | solution.py:582
  257.2 9.7 %add_convert_fusion.v_ref = bf16[4096,768]{1,0:T(8,128)(2,1)} fusion(f32[768]{0:T(1024)S(1)} %add.139, bf16[4096,768]{1,0:T(8,128)(2,1)} %bitcast.133, bf16[768,768]{1,0:T(8,128)(2,1)S(1)} %bitcast.118), kind=kOutput, calls=%fused_computation | convolution fusion | flops 4838129664 | bytes 13765632 | tf_op jit(solution)/shard_map/dot_general | solution.py:583
  268.2 21.0 %shard_map.306 = (f32[128,768]{1,0:T(8,128)}, f32[3,512,128]{2,1,0:T(8,128)}, f32[3,8,128]{2,1,0:T(8,128)}) custom-call(bf16[128,768]{1,0:T(8,128)(2,1)} %constant_dynamic-slice_fusion.2.q_ref, bf16[4096,768]{1,0:T(8,128)(2,1)} %convolution_convert_fusion.k_ref, bf16[4096,768]{1,0:T(8,128)(2,1)} %add_convert_fusion.v_ref, f32[1,4096]{1,0:T(1,128)} %compare_select_fusion.bias_ref), custom_call_target="tpu_custom_call" | custom-call | tf_op jit(solution)/shard_map/pallas_call | solution.py:461
  289.2 1.4 fusion.43
  290.9 8.6 %multiply_convert_fusion = (bf16[128,3072]{1,0:T(8,128)(2,1)S(1)}, f32[128,3072]{1,0:T(8,128)}, f32[128,3072]{1,0:T(8,128)}) fusion(f32[3072]{0:T(1024)S(1)} %add.150, bf16[768,3072]{1,0:T(8,128)(2,1)} %bitcast.115, f32[128,768]{1,0:T(8,128)S(1)} %get-tuple-element.109, f32[768]{0:T(1024)S(1)} %add.147, f32[768]{0:T(1024)S(1)} %mul.158, ...), kind=kOutput, calls=%fused_computation.12 | convolution fusion | flops 630423552 | bytes 9063424 | tf_op jit(solution)/shard_map/dot_general | solution.py:595
  299.4 3.2 fusion.44
  304.1 5.6 %convert_reduce_fusion = (f32[3072]{0:T(1024)}, bf16[128,3072]{1,0:T(8,128)(2,1)S(1)}) fusion(f32[128,3072]{1,0:T(8,128)} %get-tuple-element.90, f32[128,3072]{1,0:T(8,128)} %get-tuple-element.110, bf16[3072,768]{1,0:T(8,128)(2,1)} %bitcast.111, f32[128,768]{1,0:T(8,128)S(1)} %get-tuple-element.88, f32[128]{0:T(128)S(1)} %negate_multiply_fusion.2), kind=kOutput, calls=%fused_computation.10 | convolution fusion | flops 610464768 | bytes 9056768 | tf_op jit(solution)/shard_map/td,fd->tf/dot_general | solution.py:604
  309.7 5.0 multiply_reduce_fusion
  316.2 16.1 %shard_map.307 = (bf16[128,768]{1,0:T(8,128)(2,1)}, f32[3,8,128]{2,1,0:T(8,128)}) custom-call(bf16[128,768]{1,0:T(8,128)(2,1)} %constant_dynamic-slice_fusion.2.q_ref, bf16[4096,768]{1,0:T(8,128)(2,1)} %convolution_convert_fusion.k_ref, bf16[4096,768]{1,0:T(8,128)(2,1)} %add_convert_fusion.v_ref, f32[1,4096]{1,0:T(1,128)} %compare_select_fusion.bias_ref, ...), custom_call_target="tpu_custom_call" | custom-call | tf_op jit(solution)/shard_map/pallas_call | solution.py:501
  332.4 1.5 convolution_add_fusion.3
  333.8 1.8 constant_dynamic-slice_fusion
  337.0 46.8 %shard_map.308 = (bf16[2,4,4,128,768]{4,3,2,1,0:T(8,128)(2,1)}, f32[2,4,4,32,128]{4,3,2,1,0:T(8,128)}) custom-call(bf16[128,768]{1,0:T(8,128)(2,1)} %convolution_convert_fusion.4.g_ref.refs_0_, f32[32,128]{1,0:T(8,128)} %pad_maximum_fusion.refs_1_), custom_call_target="tpu_custom_call" | custom-call | tf_op jit(solution)/shard_map/pallas_call | solution.py:201
  383.8 1.4 copy.46
  386.9 18.0 %shard_map.309 = (bf16[128,768]{1,0:T(8,128)(2,1)}, bf16[128,768]{1,0:T(8,128)(2,1)}) custom-call(bf16[128,768]{1,0:T(8,128)(2,1)} %get-tuple-element.117.k_ref, bf16[128,768]{1,0:T(8,128)(2,1)} %get-tuple-element.116.v_ref, f32[128,128]{1,0:T(8,128)} %broadcast_in_dim.64.bias_ref, bf16[4096,768]{1,0:T(8,128)(2,1)} %add_convert_fusion.1.q_ref, ...), custom_call_target="tpu_custom_call" | custom-call | tf_op jit(solution)/shard_map/pallas_call | solution.py:540
  404.9 1.6 convolution_add_fusion.2
  406.6 1.3 fusion.6
  408.1 3.6 convolution_convert_fusion.3.g0
  411.7 3.7 convolution_convert_fusion.2.g1
  415.4 3.6 convolution_convert_fusion.1.g2
  419.6 2.3 copy-done
  421.9 2.3 copy-done.1
  424.2 2.3 copy-done.2
  426.6 96.0 %shard_map.310 = (bf16[3,4,384,768]{3,2,1,0:T(8,128)(2,1)}, f32[40,128]{1,0:T(8,128)S(1)}) custom-call(bf16[4,768,768]{2,1,0:T(8,128)(2,1)S(1)} %copy-done.2, bf16[768,3072]{1,0:T(8,128)(2,1)S(1)} %copy-done, bf16[3072,768]{1,0:T(8,128)(2,1)S(1)} %copy-done.1, f32[2,40,128]{2,1,0:T(8,128)S(1)} %bitcast.107), custom_call_target="tpu_custom_call" | custom-call | tf_op jit(solution)/shard_map/pallas_call | solution.py:389
  522.6 9.5 %convert_element_type.90 = f32[3,4,384,768]{3,2,1,0:T(8,128)} convert(bf16[3,4,384,768]{3,2,1,0:T(8,128)(2,1)} %get-tuple-element.53) | non-fusion elementwise | flops 3538944 | bytes 21233664 | tf_op jit(solution)/shard_map/convert_element_type | solution.py:655
  532.0 4.6 slice_bitcast_fusion.1
  537.2 4.8 slice_bitcast_fusion
  542.1 6.1 %copy.39 = f32[384,4,768]{0,2,1:T(8,128)} copy(f32[384,4,768]{2,0,1:T(8,128)} %slice_bitcast_fusion) | data formatting | bytes 9437184 | tf_op jit(solution)/shard_map/transpose | solution.py:668
  548.1 6.0 %copy.40 = f32[384,3072]{1,0:T(8,128)} copy(f32[384,3072]{0,1:T(8,128)} %bitcast.108) | data formatting | bytes 9437184
  554.7 4.3 slice.166
  (129 shorter events, 17.6 us)
Async XLA Ops:
  236.5 10.9 %copy-start.10 = (bf16[2,384,768]{2,1,0:T(8,128)(2,1)S(1)}, bf16[2,384,768]{2,1,0:T(8,128)(2,1)}, u32[]{:S(2)}) copy-start(bf16[2,384,768]{2,1,0:T(8,128)(2,1)} %get-tuple-element.39) | copy-start | bytes 3538948
  247.4 9.8 %copy-start.8 = (bf16[2,384,768]{2,1,0:T(8,128)(2,1)S(1)}, bf16[2,384,768]{2,1,0:T(8,128)(2,1)}, u32[]{:S(2)}) copy-start(bf16[2,384,768]{2,1,0:T(8,128)(2,1)} %get-tuple-element.40) | copy-start | bytes 3538948
  268.2 21.0 %copy-start.3 = (bf16[2,384,768]{2,1,0:T(8,128)(2,1)S(1)}, bf16[2,384,768]{2,1,0:T(8,128)(2,1)}, u32[]{:S(2)}) copy-start(bf16[2,384,768]{2,1,0:T(8,128)(2,1)} %get-tuple-element.42) | copy-start | bytes 3538948
  268.2 21.0 %copy-start.15 = (bf16[1,128,768]{2,1,0:T(8,128)(2,1)S(1)}, bf16[1,128,768]{2,1,0:T(8,128)(2,1)}, u32[]{:S(2)}) copy-start(bf16[1,128,768]{2,1,0:T(8,128)(2,1)} %param.18) | copy-start | bytes 589828
  290.9 23.9 %copy-start.20 = (f32[128]{0:T(128)}, f32[128]{0:T(128)S(1)}, u32[]{:S(2)}) copy-start(f32[128]{0:T(128)S(1)} %fusion.32) | copy-start | bytes 1540
  299.4 3.5 copy-start.7
  304.1 5.6 %copy-start.25 = (f32[128]{0:T(128)}, f32[128]{0:T(128)S(1)}, u32[]{:S(2)}) copy-start(f32[128]{0:T(128)S(1)} %negate_multiply_fusion.2) | copy-start | bytes 1540
  309.7 5.0 copy-start.5
  315.0 17.3 %copy-start.23 = (f32[128]{0:T(128)}, f32[128]{0:T(128)S(1)}, u32[]{:S(2)}) copy-start(f32[128]{0:T(128)S(1)} %negate_multiply_fusion.1) | copy-start | bytes 1540
  316.2 16.1 %copy-start.12 = (bf16[2,384,768]{2,1,0:T(8,128)(2,1)S(1)}, bf16[2,384,768]{2,1,0:T(8,128)(2,1)}, u32[]{:S(2)}) copy-start(bf16[2,384,768]{2,1,0:T(8,128)(2,1)} %get-tuple-element.37) | copy-start | bytes 3538948
  332.3 4.0 copy-start.28
  332.3 4.0 copy-start.27
  386.9 18.0 %copy-start.11 = (bf16[2,384,768]{2,1,0:T(8,128)(2,1)S(1)}, bf16[2,384,768]{2,1,0:T(8,128)(2,1)}, u32[]{:S(2)}) copy-start(bf16[2,384,768]{2,1,0:T(8,128)(2,1)} %get-tuple-element.39) | copy-start | bytes 3538948
  404.9 1.6 copy-start.9
  404.9 1.6 copy-start.14
  406.5 1.4 copy-start.4
  406.5 1.4 copy-start.24
  406.6 1.5 copy-start.13
  406.6 1.5 copy-start.16
  406.6 1.5 copy-start.17
  408.1 3.7 copy-start.6
  408.1 3.6 copy-start.21
  411.7 3.7 copy-start.26
  415.4 3.6 copy-start.22
  415.4 3.7 copy-start.19
  415.4 3.8 copy-start.18
  419.5 2.3 copy-start
  421.9 2.3 copy-start.1
  424.2 2.3 copy-start.2
